TPU v7x, 1024 devices: a whole 4x8x16 slice. The times are simulated.
1024 devices in a mesh: fsdp: 64 (over x, z), tensor: 16 (over y, core).
Axes of the slice: x: 4, y: 8, z: 16, core: 2. Of those that a mesh axis runs over, the one named last changes fastest.
Arguments:
- weights: bfloat16 [26624, 8192], P('fsdp', 'tensor'), may hold values from -3 to 3
- momentum: float32 [26624, 8192], P('fsdp', 'tensor'), may hold values from -540 to 540
- gradient: bfloat16 [26624, 8192], P('fsdp', 'tensor'), may hold values from -3 to 3
- right_factor: float32 [8192, 256], P('tensor'), may hold values from -0.0625 to 0.0625
Outputs:
- new_weights: bfloat16 [26624, 8192], P('fsdp', 'tensor')
- new_momentum: float32 [26624, 8192], P('fsdp', 'tensor')
- new_right: float32 [8192, 256], P('tensor')
All inputs are finite; a program needn't handle non-finite values.
Results may differ from a plain program's by a relative error of at most 0.001.
Values sent between devices are 32-bit elements; how exact they have to be, the bound alone decides.
No kernel may reach another device: no remote copies, remote signals or barrier semaphores. Data moves between devices by JAX's collectives and lax.ppermute only.
A program may use at most 32 MiB of HBM per device.

v0:
```python
import jax
import jax.numpy as jnp
from jax import lax
from jax.sharding import PartitionSpec as P

ROWS = 26624
COLS = 8192
RANK = 256


def product(left_side, right_side):
    return jnp.dot(
        left_side, right_side, precision=lax.Precision.HIGHEST, preferred_element_type=jnp.float32
    )


def orthonormal(left, gram):
    lower = jnp.linalg.cholesky(gram)
    return jax.scipy.linalg.solve_triangular(lower, left.T, lower=True).T


def on_device(weights, momentum, gradient, right_factor):
    buffer = momentum + gradient.astype(jnp.float32)
    left = lax.psum(product(buffer, right_factor), "tensor")
    gram = lax.psum(product(left.T, left), "fsdp")
    basis = orthonormal(left, gram)
    right = lax.psum(product(buffer.T, basis), "fsdp")
    norms_sq = lax.psum(jnp.sum(right * right, axis=0), "tensor")
    new_right = right / (jnp.sqrt(norms_sq) + 1e-06)
    new_momentum = buffer - 0.05 * product(basis, right.T)
    factor = 0.2 * (ROWS * COLS / RANK) ** 0.5
    new_weights = (weights.astype(jnp.float32) - factor * product(basis, new_right.T)).astype(
        jnp.bfloat16
    )
    return (new_weights, new_momentum, new_right)


def solution(mesh):
    in_specs = (P("fsdp", "tensor"), P("fsdp", "tensor"), P("fsdp", "tensor"), P("tensor", None))
    out_specs = (P("fsdp", "tensor"), P("fsdp", "tensor"), P("tensor", None))
    return jax.shard_map(
        on_device, mesh=mesh, in_specs=in_specs, out_specs=out_specs, check_vma=False
    )
```

profile of v0, /device:TPU:1, one launch (start us, length us, event | category | flops | bytes accessed | tf_op | source)
XLA Modules:
  0.0 796.7 jit_solution(12381748911403091440)
XLA Ops:
  7.2 0.0 copy-start
  7.2 0.0 all-reduce.5.cloned.1.call-start
  7.2 1.0 copy-done
  8.2 2.9 fusion.4
  11.1 0.0 all-reduce.5.cloned.1.call-update
  11.1 0.0 all-reduce.7.cloned.1.call-start
  11.2 132.8 %all-reduce.5.cloned.1.call-done = f32[416,256]{1,0:T(8,128)} async-done(((f32[416,256]{1,0:T(8,128)}), f32[416,256]{1,0:T(8,128)}) %all-reduce.5.cloned.1.call-update) | async-done | bytes 426000 | tf_op jit(solution)/shard_map/psum | solution.py:24
  144.0 2.8 fusion.17
  146.8 0.0 all-reduce.7.cloned.1.call-update
  146.8 0.0 all-reduce.9.cloned.1.call-start
  146.9 265.7 %all-reduce.7.cloned.1.call-done = f32[256,256]{0,1:T(8,128)} async-done(((f32[256,256]{0,1:T(8,128)}), f32[256,256]{0,1:T(8,128)}) %all-reduce.7.cloned.1.call-update) | async-done | bytes 262160 | tf_op jit(solution)/shard_map/psum | solution.py:25
  412.6 0.0 copy-start.6
  412.6 1.1 copy.8
  413.7 0.0 copy-done.6
  413.8 11.7 %cholesky.50 = f32[128,128]{1,0:T(8,128)S(1)} custom-call(f32[128,128]{1,0:T(8,128)S(1)} %cholesky.118), custom_call_target="Cholesky" | custom-call | tf_op jit(solution)/shard_map/jit(cholesky)/cholesky | solution.py:18
  425.6 9.8 %custom-call.15 = f32[1,128,128]{1,2,0:T(8,128)S(1)} custom-call(f32[1,128,128]{2,1,0:T(8,128)S(1)} %get-tuple-element.24), custom_call_target="InvertDiagBlocksLowerTriangular" | custom-call | tf_op jit(solution)/shard_map/jit(cholesky)/cholesky | solution.py:18
  435.4 0.2 constant_dynamic-update-slice_fusion.1
  435.6 0.3 convolution_subtract_fusion.1
  435.9 11.7 %cholesky.105 = f32[128,128]{1,0:T(8,128)S(1)} custom-call(f32[128,128]{1,0:T(8,128)S(1)} %convolution_subtract_fusion.1), custom_call_target="Cholesky" | custom-call | tf_op jit(solution)/shard_map/jit(cholesky)/cholesky | solution.py:18
  447.6 0.6 compare_reduce_fusion
  449.6 0.0 copy-start.4
  449.6 0.1 triangular_solve.57
  449.7 4.1 while.1
  449.8 0.6 fusion.28
  450.4 1.4 bitcast_dynamic-update-slice_fusion.2
  451.8 0.6 fusion.28
  452.4 1.4 bitcast_dynamic-update-slice_fusion.2
  453.8 0.0 copy-start.1
  453.8 19.7 %custom-call.16 = f32[2,128,128]{1,2,0:T(8,128)S(1)} custom-call(f32[2,128,128]{2,1,0:T(8,128)S(1)} %get-tuple-element.10), custom_call_target="InvertDiagBlocksLowerTriangular" | custom-call | tf_op jit(solution)/shard_map/jit(_solve_triangular)/triangular_solve | solution.py:19
  473.5 0.0 copy-done.4
  473.5 0.3 fusion.6
  473.9 0.0 copy-start.3
  473.9 0.3 convolution_subtract_fusion
  474.2 0.3 fusion.9
  474.6 0.0 copy-done.1
  474.6 0.3 copy-done.3
  474.9 2.7 fusion.3
  477.5 0.0 all-reduce.9.cloned.1.call-update
  477.6 273.5 %all-reduce.9.cloned.1.call-done = f32[512,256]{1,0:T(8,128)} async-done(((f32[512,256]{1,0:T(8,128)}), f32[512,256]{1,0:T(8,128)}) %all-reduce.9.cloned.1.call-update) | async-done | bytes 524304 | tf_op jit(solution)/shard_map/psum | solution.py:27
  751.0 0.0 copy-start.2
  751.0 1.2 multiply_reduce_fusion
  752.2 33.5 %psum.31 = f32[256]{0:T(256)S(1)} all-reduce(f32[256]{0:T(256)S(1)} %multiply_reduce_fusion), channel_id=1, replica_groups=mesh['fsdp'=64,'tensor'=16] {'tensor'}, use_global_device_ids=true, to_apply=%region_8.9 | all-reduce | flops 256 | bytes 2048 | tf_op jit(solution)/shard_map/psum | solution.py:28
  785.7 0.0 copy-done.2
  785.7 0.0 copy-start.7
  785.8 1.0 copy-done.7
  786.8 1.6 fusion.2
  788.4 0.0 copy-done.5
  788.4 1.8 fusion
  (13 shorter events, 0.2 us)
Async XLA Ops:
  7.2 1.0 copy-start
  7.2 136.8 %all-reduce.5.cloned.1.call-start = ((), (), s32[]{:S(2)}) async-start(), calls=%async_computation | async-start | bytes 851968 | tf_op jit(solution)/shard_map/psum | solution.py:24
  11.1 401.5 %all-reduce.7.cloned.1.call-start = ((), (), s32[]{:S(2)}) async-start(), calls=%async_computation.1 | async-start | bytes 524288 | tf_op jit(solution)/shard_map/psum | solution.py:25
  146.8 604.2 %all-reduce.9.cloned.1.call-start = ((), (), s32[]{:S(2)}) async-start(), calls=%async_computation.2 | async-start | bytes 1048576 | tf_op jit(solution)/shard_map/psum | solution.py:27
  412.6 1.2 copy-start.6
  449.6 23.9 %copy-start.4 = (f32[416,256]{1,0:T(8,128)S(1)}, f32[416,256]{1,0:T(8,128)}, u32[]{:S(2)}) copy-start(f32[416,256]{1,0:T(8,128)} %all-reduce.5.cloned.1.call-done) | copy-start | bytes 1277956
  453.8 20.7 %copy-start.1 = (f32[416,512]{1,0:T(8,128)S(1)}, f32[416,512]{1,0:T(8,128)}, u32[]{:S(2)}) copy-start(f32[416,512]{1,0:T(8,128)} %param.5) | copy-start | bytes 2555908
  473.9 1.0 copy-start.3
  751.0 34.7 %copy-start.2 = (f32[512,256]{1,0:T(8,128)S(1)}, f32[512,256]{1,0:T(8,128)}, u32[]{:S(2)}) copy-start(f32[512,256]{1,0:T(8,128)} %all-reduce.9.cloned.1.call-done) | copy-start | bytes 1572868
  785.7 1.0 copy-start.7
  786.8 1.7 copy-start.5
Sparse Core Ops, SparseCore 0:
  11.2 132.6 all-reduce.4
  148.4 264.1 all-reduce.6
  477.7 273.2 all-reduce.8
where the time goes:
time: 797 us
  waiting for transfers between devices  672 us (84%)
  other arithmetic  54.9 us (7%)
  blocking collectives  33.5 us (4%)
  between operations  15.2 us (2%)
  matrix products  13.3 us (2%)
    psum x1, waiting for transfers between devices, on_device(): right = lax.psum(product(buffer.T, basis), 'fsdp')  273 us
    psum x1, waiting for transfers between devices, on_device(): gram = lax.psum(product(left.T, left), 'fsdp')  266 us
    psum x1, waiting for transfers between devices, on_device(): left = lax.psum(product(buffer, right_factor), 'tensor')  133 us
    another operation x6, other arithmetic, orthonormal(): lower = jnp.linalg.cholesky(gram)  34 us
    psum x1, blocking collectives, on_device(): norms_sq = lax.psum(jnp.sum(right * right, axis=0), 'tensor')  33.5 us
    another operation x3, other arithmetic, orthonormal(): return jax.scipy.linalg.solve_triangular(lower, left.T, lower=True).T  19.7 us
  transfers between devices with their start and end apart: 3, of which 3 were waited for; matrix products, arithmetic and copies ran while one was open for 0% of the time, Pallas kernels for 0%

commit v1 on v0

v1 whole, which is shorter than its diff:
```python
import jax
import jax.numpy as jnp
from jax import lax
from jax.sharding import PartitionSpec as P

ROWS = 26624
COLS = 8192
RANK = 256
X = 4
Z = 16
T = 16
FACTOR = 0.2 * (ROWS * COLS / RANK) ** 0.5

GROUPS_X = [[x * Z + z for x in range(X)] for z in range(Z)]
GROUPS_Z = [[x * Z + z for z in range(Z)] for x in range(X)]


def dot(left_side, right_side, left_dim, right_dim, precision=lax.Precision.HIGHEST):
    return lax.dot_general(
        left_side,
        right_side,
        (((left_dim,), (right_dim,)), ((), ())),
        precision=precision,
        preferred_element_type=jnp.float32,
    )


def exchange(blocks, axis, groups=None):
    return lax.all_to_all(blocks, axis, 0, 0, axis_index_groups=groups)


def reduce_scatter(array, parts, axis, groups=None):
    blocks = array.reshape(parts, array.shape[0] // parts, array.shape[1])
    return jnp.sum(exchange(blocks, axis, groups), axis=0)


def gather(array, parts, axis, groups=None):
    blocks = exchange(jnp.broadcast_to(array, (parts, *array.shape)), axis, groups)
    return blocks.reshape(parts * array.shape[0], array.shape[1])


def inverse_factor(gram):
    lower = jnp.linalg.cholesky(gram)
    eye = jnp.eye(RANK, dtype=jnp.float32)
    return jax.scipy.linalg.solve_triangular(lower, eye, lower=True)


def on_device(weights, momentum, gradient, right_factor):
    buffer = momentum + gradient.astype(jnp.float32)
    part = dot(right_factor, buffer, 0, 1)
    left_t = lax.all_gather(reduce_scatter(part, T, "tensor"), "tensor", tiled=True)
    gram = dot(left_t, left_t, 1, 1)
    raw = dot(buffer, left_t, 0, 1)
    half = RANK // 2
    both = jnp.concatenate(
        [raw, jnp.concatenate([gram[:, :half], gram[:, half:]], axis=0)], axis=1
    )
    both = reduce_scatter(both, X, "fsdp", GROUPS_X)
    both = reduce_scatter(both, Z, "fsdp", GROUPS_Z)
    both = gather(both, Z, "fsdp", GROUPS_Z)
    both = gather(both, X, "fsdp", GROUPS_X)
    raw = both[:, :RANK]
    gram = jnp.concatenate([both[:RANK, RANK:], both[RANK:, RANK:]], axis=1)
    inverse = inverse_factor(gram)
    basis_t = dot(inverse, left_t, 1, 0)
    right = dot(raw, inverse, 1, 1)
    norms = jnp.sum(right * right, axis=0, keepdims=True)
    norms_sq = jnp.sum(exchange(jnp.broadcast_to(norms, (T, 1, RANK)), "tensor"), axis=0)
    new_right = right / (jnp.sqrt(norms_sq) + 1e-06)
    new_momentum = buffer - 0.05 * dot(basis_t, right, 0, 1)
    new_weights = (weights.astype(jnp.float32) - FACTOR * dot(basis_t, new_right, 0, 1)).astype(
        jnp.bfloat16
    )
    return (new_weights, new_momentum, new_right)


def solution(mesh):
    in_specs = (P("fsdp", "tensor"), P("fsdp", "tensor"), P("fsdp", "tensor"), P("tensor", None))
    out_specs = (P("fsdp", "tensor"), P("fsdp", "tensor"), P("tensor", None))
    return jax.shard_map(
        on_device, mesh=mesh, in_specs=in_specs, out_specs=out_specs, check_vma=False
    )
```

time: 797 us -> 215 us (0.27)
  waiting for transfers between devices: 672 us -> 13.6 us
  blocking collectives: 33.5 us -> 108 us
  starting transfers between devices: 0.12 us -> 15 us
  between operations: 15.2 us -> 2.25 us
    psum x3 -> x0, waiting for transfers between devices: 672 us -> none  [the longest x1 273 us: on_device(): right = lax.psum(product(buffer.T, basis), 'fsdp')]
    all_to_all x0 -> x4, blocking collectives: none -> 92.3 us  [exchange(): return lax.all_to_all(blocks, axis, 0, 0, axis_index_groups=groups)]
    psum x1 -> x0, blocking collectives: 33.5 us -> none  [on_device(): norms_sq = lax.psum(jnp.sum(right * right, axis=0), 'tensor')]
    all_gather x0 -> x1, blocking collectives: none -> 16 us  [on_device(): lax.all_gather(reduce_scatter(part, T, 'tensor'), 'tensor', tiled=True)]
    all_to_all x0 -> x2, starting transfers between devices: none -> 15 us  [exchange(): return lax.all_to_all(blocks, axis, 0, 0, axis_index_groups=groups)]
    all_to_all x0 -> x2, waiting for transfers between devices: none -> 13.6 us  [exchange(): return lax.all_to_all(blocks, axis, 0, 0, axis_index_groups=groups)]
  transfers between devices with their start and end apart: 3 -> 2, of which waited for: 3 -> 2; matrix products, arithmetic and copies ran while one was open for 0% -> 1% of each run, Pallas kernels for 0% -> 0%
where the time goes in v1:
time: 215 us
  blocking collectives  108 us (50%)
  other arithmetic  54.3 us (25%)
  starting transfers between devices  15 us (7%)
  waiting for transfers between devices  13.6 us (6%)
  matrix products  11.6 us (5%)
  local copies, waits for them, and re-layouts  9.69 us (5%)
  between operations  2.25 us (1%)
    all_to_all x4, blocking collectives, exchange(): return lax.all_to_all(blocks, axis, 0, 0, axis_index_groups=groups)  92.3 us
    another operation x6, other arithmetic, inverse_factor(): lower = jnp.linalg.cholesky(gram)  34 us
    another operation x3, other arithmetic, inverse_factor(): return jax.scipy.linalg.solve_triangular(lower, eye, lower=True)  19.9 us
    all_gather x1, blocking collectives, on_device(): lax.all_gather(reduce_scatter(part, T, 'tensor'), 'tensor', tiled=True)  16 us
    all_to_all x2, starting transfers between devices, exchange(): return lax.all_to_all(blocks, axis, 0, 0, axis_index_groups=groups)  15 us
    all_to_all x2, waiting for transfers between devices, exchange(): return lax.all_to_all(blocks, axis, 0, 0, axis_index_groups=groups)  13.6 us
    dot_general x7, matrix products, dot(): lax.dot_general(left_side, right_side, (((left_dim,), (right_dim,)), ((),...  10.3 us
  transfers between devices with their start and end apart: 2, of which 2 were waited for; matrix products, arithmetic and copies ran while one was open for 1% of the time, Pallas kernels for 0%

profile of v1, /device:TPU:1, one launch (start us, length us, event | category | flops | bytes accessed | tf_op | source)
XLA Modules:
  0.0 214.8 jit_solution(16383907923471554270)
XLA Ops:
  0.6 0.0 copy-start
  0.6 1.0 copy-done
  1.7 2.1 convolution_bitcast_fusion
  3.8 0.2 copy.41
  4.0 33.9 %all_to_all.30 = f32[16,16,416]{2,1,0:T(8,128)S(1)} all-to-all(f32[16,16,416]{2,1,0:T(8,128)S(1)} %bitcast.55), channel_id=1, replica_groups=mesh['fsdp'=64,'tensor'=16] {'tensor'}, dimensions={0} | all-to-all | bytes 851968 | tf_op jit(solution)/shard_map/all_to_all | solution.py:29
  38.0 0.0 copy-start.1
  38.0 16.0 %all_gather.3 = f32[256,416]{1,0:T(8,128)S(1)} all-gather(f32[16,416]{1,0:T(8,128)S(1)} %reduce_sum.45), channel_id=1, replica_groups=mesh['fsdp'=64,'tensor'=16] {'tensor'}, dimensions={0}, use_global_device_ids=true | all-gather | bytes 452608 | tf_op jit(solution)/shard_map/all_gather | solution.py:51
  54.0 0.6 fusion.20
  54.7 0.0 copy-done.1
  54.7 0.4 copy-done.2
  55.1 1.1 fusion.5
  56.2 0.1 copy_bitcast_fusion.1
  56.2 14.4 %all_to_all.31 = f32[4,128,384]{1,2,0:T(8,128)S(1)} all-to-all(f32[4,128,384]{1,2,0:T(8,128)S(1)} %copy_bitcast_fusion.1), channel_id=1, replica_groups={{0,256,512,768},{16,272,528,784},{32,288,544,800},{48,304,560,816},{64,..., dimensions={0} | all-to-all | bytes 1572864 | tf_op jit(solution)/shard_map/all_to_all | solution.py:29
  70.7 0.1 copy.46
  70.8 23.9 %all_to_all.32 = f32[16,8,384]{2,1,0:T(8,128)S(1)} all-to-all(f32[16,8,384]{2,1,0:T(8,128)S(1)} %bitcast.56), channel_id=1, replica_groups={{0,16,32,48,64,80,96,112,128,144,160,176,192,208,224,240},{256,272,288,..., dimensions={0} | all-to-all | bytes 393216 | tf_op jit(solution)/shard_map/all_to_all | solution.py:29
  94.8 20.1 %all_to_all.33 = f32[16,8,384]{2,1,0:T(8,128)S(1)} all-to-all(f32[16,8,384]{2,1,0:T(8,128)S(1)} %broadcast_in_dim.12), channel_id=1, replica_groups={{0,16,32,48,64,80,96,112,128,144,160,176,192,208,224,240},{256,272,288,..., dimensions={0} | all-to-all | bytes 393216 | tf_op jit(solution)/shard_map/all_to_all | solution.py:29
  114.9 0.1 copy.47
  115.0 0.9 broadcast_in_dim.13
  115.9 3.7 %all-to-all-start.4 = ((f32[4,128,384]{1,2,0:T(8,128)}), f32[4,128,384]{1,2,0:T(8,128)S(1)}, u32[]{:S(2)}, u32[]{:S(2)}) async-start(f32[4,128,384]{1,2,0:T(8,128)} %broadcast_in_dim.13), calls=%async_computation.4 | async-start | bytes 1572864 | tf_op jit(solution)/shard_map/all_to_all | solution.py:29
  119.7 8.1 %all-to-all-done.4 = f32[4,128,384]{1,2,0:T(8,128)S(1)} async-done(((f32[4,128,384]{1,2,0:T(8,128)}), f32[4,128,384]{1,2,0:T(8,128)S(1)}, u32[]{:S(2)}, u32[]{:S(2)}) %all-to-all-start.4) | async-done | bytes 786464 | tf_op jit(solution)/shard_map/all_to_all | solution.py:29
  127.7 0.1 copy_bitcast_fusion
  127.8 0.0 copy-start.3
  127.9 0.9 copy-done.3
  128.8 0.1 copy.49
  129.0 11.7 %cholesky.50 = f32[128,128]{1,0:T(8,128)S(1)} custom-call(f32[128,128]{1,0:T(8,128)S(1)} %cholesky.118), custom_call_target="Cholesky" | custom-call | tf_op jit(solution)/shard_map/jit(cholesky)/cholesky | solution.py:43
  140.7 9.8 %custom-call.15 = f32[1,128,128]{1,2,0:T(8,128)S(1)} custom-call(f32[1,128,128]{2,1,0:T(8,128)S(1)} %get-tuple-element.28), custom_call_target="InvertDiagBlocksLowerTriangular" | custom-call | tf_op jit(solution)/shard_map/jit(cholesky)/cholesky | solution.py:43
  150.6 0.2 constant_dynamic-update-slice_fusion.1
  150.8 0.3 convolution_subtract_fusion.1
  151.0 11.7 %cholesky.105 = f32[128,128]{1,0:T(8,128)S(1)} custom-call(f32[128,128]{1,0:T(8,128)S(1)} %convolution_subtract_fusion.1), custom_call_target="Cholesky" | custom-call | tf_op jit(solution)/shard_map/jit(cholesky)/cholesky | solution.py:43
  162.8 0.7 compare_reduce_fusion
  164.9 0.1 triangular_solve.63
  165.0 4.1 %while.1 = (s32[]{:T(128)}, f32[256,256]{1,0:T(8,128)S(1)}, s32[2,2]{1,0:T(2,128)S(1)}, f32[2,128,128]{2,1,0:T(8,128)S(1)}, s32[]{:T(128)}) while((s32[]{:T(128)}, f32[256,256]{1,0:T(8,128)S(1)}, s32[2,2]{1,0:T(2,128)S(1)}, f32[2,128,128]{2,1,0:T(8,128)S(1)}, s32[]{:T(128)}) %tuple.30), condition=%wide.while_cond, body=%wide.while_body.sunk | while | flops 2 | bytes 131181 | solution.py:45
  165.0 0.6 fusion.36
  165.6 1.4 bitcast_dynamic-update-slice_fusion.2
  167.0 0.6 fusion.36
  167.6 1.4 bitcast_dynamic-update-slice_fusion.2
  169.1 19.9 %custom-call.16 = f32[2,128,128]{1,2,0:T(8,128)S(1)} custom-call(f32[2,128,128]{2,1,0:T(8,128)S(1)} %get-tuple-element.10), custom_call_target="InvertDiagBlocksLowerTriangular" | custom-call | tf_op jit(solution)/shard_map/jit(_solve_triangular)/triangular_solve | solution.py:45
  189.0 0.3 fusion.8
  189.2 0.3 convolution_subtract_fusion
  189.5 0.3 fusion.11
  189.8 2.1 multiply_reduce_fusion
  191.9 1.0 fusion.7
  192.9 0.6 broadcast_in_dim.14
  193.5 11.3 %all-to-all-start.5 = ((f32[16,1,256]{2,1,0:T(1,128)}), f32[16,1,256]{2,1,0:T(1,128)S(1)}, u32[]{:S(2)}, u32[]{:S(2)}) async-start(f32[16,1,256]{2,1,0:T(1,128)} %broadcast_in_dim.14), calls=%async_computation.5 | async-start | bytes 32768 | tf_op jit(solution)/shard_map/all_to_all | solution.py:29
  204.8 1.8 fusion
  206.6 5.5 %all-to-all-done.5 = f32[16,1,256]{2,1,0:T(1,128)S(1)} async-done(((f32[16,1,256]{2,1,0:T(1,128)}), f32[16,1,256]{2,1,0:T(1,128)S(1)}, u32[]{:S(2)}, u32[]{:S(2)}) %all-to-all-start.5) | async-done | bytes 16416 | tf_op jit(solution)/shard_map/all_to_all | solution.py:29
  212.2 1.0 copy-done.5
  213.2 1.6 fusion.2
  (25 shorter events, 0.5 us)
Async XLA Ops:
  0.6 1.0 copy-start
  38.0 16.7 %copy-start.1 = (f32[416,512]{1,0:T(8,128)S(1)}, f32[416,512]{1,0:T(8,128)}, u32[]{:S(2)}) copy-start(f32[416,512]{1,0:T(8,128)} %param.5) | copy-start | bytes 2555908
  54.0 1.0 copy-start.2
  115.9 11.8 %all-to-all-start.4 = ((f32[4,128,384]{1,2,0:T(8,128)}), f32[4,128,384]{1,2,0:T(8,128)S(1)}, u32[]{:S(2)}, u32[]{:S(2)}) async-start(f32[4,128,384]{1,2,0:T(8,128)} %broadcast_in_dim.13), calls=%async_computation.4 | async-start | bytes 1572864 | tf_op jit(solution)/shard_map/all_to_all | solution.py:29
  127.8 0.9 copy-start.3
  193.5 18.6 %all-to-all-start.5 = ((f32[16,1,256]{2,1,0:T(1,128)}), f32[16,1,256]{2,1,0:T(1,128)S(1)}, u32[]{:S(2)}, u32[]{:S(2)}) async-start(f32[16,1,256]{2,1,0:T(1,128)} %broadcast_in_dim.14), calls=%async_computation.5 | async-start | bytes 32768 | tf_op jit(solution)/shard_map/all_to_all | solution.py:29
  212.2 1.0 copy-start.5
  213.2 1.7 copy-start.4

commit v2 on v1

--- a/solution.py
+++ b/solution.py
@@ -1,6 +1,8 @@
 import jax
 import jax.numpy as jnp
 from jax import lax
+from jax.experimental import pallas as pl
+from jax.experimental.pallas import tpu as pltpu
 from jax.sharding import PartitionSpec as P
 
 ROWS = 26624
@@ -9,6 +11,8 @@
 X = 4
 Z = 16
 T = 16
+BLOCK = 64
+HALF = RANK // 2
 FACTOR = 0.2 * (ROWS * COLS / RANK) ** 0.5
 
 GROUPS_X = [[x * Z + z for x in range(X)] for z in range(Z)]
@@ -39,10 +43,74 @@
     return blocks.reshape(parts * array.shape[0], array.shape[1])
 
 
-def inverse_factor(gram):
-    lower = jnp.linalg.cholesky(gram)
-    eye = jnp.eye(RANK, dtype=jnp.float32)
-    return jax.scipy.linalg.solve_triangular(lower, eye, lower=True)
+def lane(group, k):
+    return jnp.broadcast_to(group[:, k : k + 1], group.shape)
+
+
+def sublane(group, k):
+    return jnp.broadcast_to(group[k : k + 1, :], group.shape)
+
+
+def eliminate(groups):
+    row = lax.broadcasted_iota(jnp.int32, groups[0].shape, 0)
+    for p in range(len(groups)):
+        rest = range(p, len(groups))
+        column = {q: [lane(groups[q], 8 * p + k) for k in range(8)] for q in rest}
+        pivots = jnp.ones_like(groups[p])
+        for k in range(8):
+            pivot = sublane(column[p][k], k)
+            pivots = jnp.where(row == k, pivot, pivots)
+            inverse = 1.0 / pivot
+            pivot_row = sublane(groups[p], k)
+            later = {j: sublane(column[p][j], k) for j in range(k + 1, 8)}
+            for q in rest:
+                ratio = column[q][k] * inverse
+                if q == p:
+                    ratio = jnp.where(row > k, ratio, 0.0)
+                groups[q] = groups[q] - ratio * pivot_row
+                for j in later:
+                    column[q][j] = column[q][j] - ratio * later[j]
+        groups[p] = groups[p] * lax.rsqrt(pivots)
+    return groups
+
+
+def factor_kernel(both_ref, inverse_ref, right_ref, norms_ref, work):
+    work[:, :HALF] = both_ref[:RANK, RANK:]
+    work[:, HALF:RANK] = both_ref[RANK:, RANK:]
+    i = lax.broadcasted_iota(jnp.int32, (RANK, RANK), 0)
+    j = lax.broadcasted_iota(jnp.int32, (RANK, RANK), 1)
+    work[:, RANK:] = jnp.where(i == j, 1.0, 0.0)
+    i = lax.broadcasted_iota(jnp.int32, (BLOCK, BLOCK), 0)
+    j = lax.broadcasted_iota(jnp.int32, (BLOCK, BLOCK), 1)
+    eye = jnp.where(i == j, 1.0, 0.0)
+    for start in range(0, RANK, BLOCK):
+        stop = start + BLOCK
+        wide = jnp.concatenate([work[start:stop, :RANK][:, start:stop], eye], axis=1)
+        groups = eliminate([wide[q : q + 8, :] for q in range(0, BLOCK, 8)])
+        block = dot(jnp.concatenate(groups, axis=0)[:, BLOCK:], work[start:stop, :], 1, 0)
+        inverse_ref[start:stop, :] = block[:, RANK:]
+        if stop < RANK:
+            work[stop:, :] = work[stop:, :] - dot(block[:, :RANK].T[stop:, :], block, 1, 0)
+    right = dot(both_ref[:, :RANK], inverse_ref[...], 1, 1)
+    right_ref[...] = right
+    norms_ref[...] = jnp.sum(right * right, axis=0, keepdims=True)
+
+
+def factor(both):
+    cols = both.shape[0]
+    return pl.pallas_call(
+        factor_kernel,
+        out_shape=(
+            jax.ShapeDtypeStruct((RANK, RANK), jnp.float32),
+            jax.ShapeDtypeStruct((cols, RANK), jnp.float32),
+            jax.ShapeDtypeStruct((1, RANK), jnp.float32),
+        ),
+        in_specs=[pl.BlockSpec(memory_space=pltpu.VMEM)],
+        out_specs=[pl.BlockSpec(memory_space=pltpu.VMEM)] * 3,
+        scratch_shapes=[pltpu.VMEM((RANK, 2 * RANK), jnp.float32)],
+        compiler_params=pltpu.CompilerParams(vmem_limit_bytes=24 * 2**20),
+        cost_estimate=pl.CostEstimate(flops=10**9, bytes_accessed=2 * 10**6, transcendentals=0),
+    )(both)
 
 
 def on_device(weights, momentum, gradient, right_factor):
@@ -51,24 +119,19 @@
     left_t = lax.all_gather(reduce_scatter(part, T, "tensor"), "tensor", tiled=True)
     gram = dot(left_t, left_t, 1, 1)
     raw = dot(buffer, left_t, 0, 1)
-    half = RANK // 2
     both = jnp.concatenate(
-        [raw, jnp.concatenate([gram[:, :half], gram[:, half:]], axis=0)], axis=1
+        [raw, jnp.concatenate([gram[:, :HALF], gram[:, HALF:]], axis=0)], axis=1
     )
     both = reduce_scatter(both, X, "fsdp", GROUPS_X)
     both = reduce_scatter(both, Z, "fsdp", GROUPS_Z)
     both = gather(both, Z, "fsdp", GROUPS_Z)
     both = gather(both, X, "fsdp", GROUPS_X)
-    raw = both[:, :RANK]
-    gram = jnp.concatenate([both[:RANK, RANK:], both[RANK:, RANK:]], axis=1)
-    inverse = inverse_factor(gram)
+    inverse, right, norms = factor(both)
+    norms_sq = jnp.sum(exchange(jnp.broadcast_to(norms, (T, 1, RANK)), "tensor"), axis=0)
     basis_t = dot(inverse, left_t, 1, 0)
-    right = dot(raw, inverse, 1, 1)
-    norms = jnp.sum(right * right, axis=0, keepdims=True)
-    norms_sq = jnp.sum(exchange(jnp.broadcast_to(norms, (T, 1, RANK)), "tensor"), axis=0)
     new_right = right / (jnp.sqrt(norms_sq) + 1e-06)
-    new_momentum = buffer - 0.05 * dot(basis_t, right, 0, 1)
-    new_weights = (weights.astype(jnp.float32) - FACTOR * dot(basis_t, new_right, 0, 1)).astype(
+    new_momentum = buffer - 0.05 * dot(basis_t, right, 0, 1, lax.Precision.HIGH)
+    new_weights = (weights.astype(jnp.float32) - FACTOR * dot(basis_t, new_right, 0, 1, lax.Precision.HIGH)).astype(
         jnp.bfloat16
     )
     return (new_weights, new_momentum, new_right)

time: 215 us -> 159 us (0.74)
  other arithmetic: 54.3 us -> 0.24 us
  blocking collectives: 108 us -> 119 us
  Pallas kernels: 0 us -> 10.3 us
  waiting for transfers between devices: 13.6 us -> 5.84 us
  local copies, waits for them, and re-layouts: 9.69 us -> 3.41 us
  matrix products: 11.6 us -> 7.63 us
  starting transfers between devices: 15 us -> 11.3 us
    another operation x9 -> x0, other arithmetic: 54 us -> none  [the longest x6 34 us: inverse_factor(): lower = jnp.linalg.cholesky(gram)]
    all_to_all x4 -> x5, blocking collectives: 92.3 us -> 103 us  [exchange(): return lax.all_to_all(blocks, axis, 0, 0, axis_index_groups=groups)]
    pallas_call x0 -> x1, Pallas kernels: none -> 10.3 us  [factor(): pl.pallas_call(factor_kernel, out_shape=(jax.ShapeDtypeStruct((RANK, RANK...]
    all_to_all x2 -> x1, waiting for transfers between devices: 13.6 us -> 5.84 us  [exchange(): return lax.all_to_all(blocks, axis, 0, 0, axis_index_groups=groups)]
    another operation x9 -> x0, local copies, waits for them, and re-layouts: 4.16 us -> none
    all_to_all x2 -> x1, starting transfers between devices: 15 us -> 11.3 us  [exchange(): return lax.all_to_all(blocks, axis, 0, 0, axis_index_groups=groups)]
    dot_general x7 -> x6, matrix products: 10.3 us -> 7.63 us  [dot(): lax.dot_general(left_side, right_side, (((left_dim,), (right_dim,)), ((),...]
  transfers between devices with their start and end apart: 2 -> 1, of which waited for: 2 -> 1; matrix products, arithmetic and copies ran while one was open for 1% -> 1% of each run, Pallas kernels for 0% -> 0%
where the time goes in v2:
time: 159 us
  blocking collectives  119 us (75%)
  starting transfers between devices  11.3 us (7%)
  Pallas kernels  10.3 us (6%)
  matrix products  7.63 us (5%)
  waiting for transfers between devices  5.84 us (4%)
  local copies, waits for them, and re-layouts  3.41 us (2%)
    all_to_all x5, blocking collectives, exchange(): return lax.all_to_all(blocks, axis, 0, 0, axis_index_groups=groups)  103 us
    all_gather x1, blocking collectives, on_device(): lax.all_gather(reduce_scatter(part, T, 'tensor'), 'tensor', tiled=True)  16 us
    all_to_all x1, starting transfers between devices, exchange(): return lax.all_to_all(blocks, axis, 0, 0, axis_index_groups=groups)  11.3 us
    pallas_call x1, Pallas kernels, factor(): pl.pallas_call(factor_kernel, out_shape=(jax.ShapeDtypeStruct((RANK, RANK...  10.3 us
    dot_general x6, matrix products, dot(): lax.dot_general(left_side, right_side, (((left_dim,), (right_dim,)), ((),...  7.63 us
    all_to_all x1, waiting for transfers between devices, exchange(): return lax.all_to_all(blocks, axis, 0, 0, axis_index_groups=groups)  5.84 us
  transfers between devices with their start and end apart: 1, of which 1 were waited for; matrix products, arithmetic and copies ran while one was open for 1% of the time, Pallas kernels for 0%

profile of v2, /device:TPU:1, one launch (start us, length us, event | category | flops | bytes accessed | tf_op | source)
XLA Modules:
  0.0 158.6 jit_solution(15199103692161914676)
XLA Ops:
  0.6 0.0 copy-start
  0.6 1.0 copy-done
  1.7 2.1 %convolution_bitcast_fusion = f32[256,416]{0,1:T(8,128)S(1)} fusion(f32[512,256]{1,0:T(8,128)S(1)} %copy-done, f32[416,512]{1,0:T(8,128)} %param.5, bf16[416,512]{1,0:T(8,128)(2,1)} %param.6), kind=kOutput, calls=%fused_computation.5 | convolution fusion | flops 654737408 | bytes 2228224 | tf_op jit(solution)/shard_map/dot_general | solution.py:23
  3.8 0.2 copy.29
  4.0 33.9 %all_to_all.30 = f32[16,16,416]{2,1,0:T(8,128)S(1)} all-to-all(f32[16,16,416]{2,1,0:T(8,128)S(1)} %bitcast.24), channel_id=1, replica_groups=mesh['fsdp'=64,'tensor'=16] {'tensor'}, dimensions={0} | all-to-all | bytes 851968 | tf_op jit(solution)/shard_map/all_to_all | solution.py:33
  38.0 0.0 copy-start.1
  38.0 16.0 %all_gather.3 = f32[256,416]{1,0:T(8,128)S(1)} all-gather(f32[16,416]{1,0:T(8,128)S(1)} %reduce_sum.36), channel_id=1, replica_groups=mesh['fsdp'=64,'tensor'=16] {'tensor'}, dimensions={0}, use_global_device_ids=true | all-gather | bytes 452608 | tf_op jit(solution)/shard_map/all_gather | solution.py:119
  54.0 0.0 copy-start.2
  54.0 0.6 fusion.5
  54.7 0.0 copy-done.1
  54.7 0.4 copy-done.2
  55.0 1.1 fusion.3
  56.2 0.1 copy_bitcast_fusion
  56.2 14.4 %all_to_all.31 = f32[4,128,384]{1,2,0:T(8,128)S(1)} all-to-all(f32[4,128,384]{1,2,0:T(8,128)S(1)} %copy_bitcast_fusion), channel_id=1, replica_groups={{0,256,512,768},{16,272,528,784},{32,288,544,800},{48,304,560,816},{64,..., dimensions={0} | all-to-all | bytes 1572864 | tf_op jit(solution)/shard_map/all_to_all | solution.py:33
  70.7 0.1 copy.34
  70.8 23.9 %all_to_all.32 = f32[16,8,384]{2,1,0:T(8,128)S(1)} all-to-all(f32[16,8,384]{2,1,0:T(8,128)S(1)} %bitcast.25), channel_id=1, replica_groups={{0,16,32,48,64,80,96,112,128,144,160,176,192,208,224,240},{256,272,288,..., dimensions={0} | all-to-all | bytes 393216 | tf_op jit(solution)/shard_map/all_to_all | solution.py:33
  94.8 20.1 %all_to_all.33 = f32[16,8,384]{2,1,0:T(8,128)S(1)} all-to-all(f32[16,8,384]{2,1,0:T(8,128)S(1)} %broadcast_in_dim.9), channel_id=1, replica_groups={{0,16,32,48,64,80,96,112,128,144,160,176,192,208,224,240},{256,272,288,..., dimensions={0} | all-to-all | bytes 393216 | tf_op jit(solution)/shard_map/all_to_all | solution.py:33
  114.9 0.1 broadcast_in_dim.10
  114.9 10.7 %all_to_all.34 = f32[4,128,384]{2,1,0:T(8,128)S(1)} all-to-all(f32[4,128,384]{2,1,0:T(8,128)S(1)} %broadcast_in_dim.10), channel_id=1, replica_groups={{0,256,512,768},{16,272,528,784},{32,288,544,800},{48,304,560,816},{64,..., dimensions={0} | all-to-all | bytes 1572864 | tf_op jit(solution)/shard_map/all_to_all | solution.py:33
  125.7 10.3 %shard_map.67 = (f32[256,256]{1,0:T(8,128)S(1)}, f32[512,256]{1,0:T(8,128)S(1)}, f32[1,256]{1,0:T(1,128)S(1)}) custom-call(f32[512,384]{1,0:T(8,128)S(1)} %bitcast.22), custom_call_target="tpu_custom_call" | custom-call | flops 1000000000 | bytes 2000000 | tf_op jit(solution)/shard_map/pallas_call | solution.py:101
  136.0 1.0 fusion.6
  136.9 0.6 broadcast_in_dim.11
  137.6 11.3 %all-to-all-start.5 = ((f32[16,1,256]{2,1,0:T(1,128)}), f32[16,1,256]{2,1,0:T(1,128)S(1)}, u32[]{:S(2)}, u32[]{:S(2)}) async-start(f32[16,1,256]{2,1,0:T(1,128)} %broadcast_in_dim.11), calls=%async_computation.5 | async-start | bytes 32768 | tf_op jit(solution)/shard_map/all_to_all | solution.py:33
  148.9 1.5 fusion
  150.4 5.8 %all-to-all-done.5 = f32[16,1,256]{2,1,0:T(1,128)S(1)} async-done(((f32[16,1,256]{2,1,0:T(1,128)}), f32[16,1,256]{2,1,0:T(1,128)S(1)}, u32[]{:S(2)}, u32[]{:S(2)}) %all-to-all-start.5) | async-done | bytes 16416 | tf_op jit(solution)/shard_map/all_to_all | solution.py:33
  156.3 0.0 copy-start.4
  156.3 1.0 copy-done.4
  157.3 0.0 copy-start.3
  157.3 1.3 fusion.2
  158.6 0.0 copy-done.3
  (8 shorter events, 0.2 us)
Async XLA Ops:
  0.6 1.0 copy-start
  38.0 16.7 %copy-start.1 = (f32[416,512]{1,0:T(8,128)S(1)}, f32[416,512]{1,0:T(8,128)}, u32[]{:S(2)}) copy-start(f32[416,512]{1,0:T(8,128)} %param.5) | copy-start | bytes 2555908
  54.0 1.0 copy-start.2
  137.6 18.6 %all-to-all-start.5 = ((f32[16,1,256]{2,1,0:T(1,128)}), f32[16,1,256]{2,1,0:T(1,128)S(1)}, u32[]{:S(2)}, u32[]{:S(2)}) async-start(f32[16,1,256]{2,1,0:T(1,128)} %broadcast_in_dim.11), calls=%async_computation.5 | async-start | bytes 32768 | tf_op jit(solution)/shard_map/all_to_all | solution.py:33
  156.3 1.0 copy-start.4
  157.3 1.3 copy-start.3

commit v3 on v2

--- a/solution.py
+++ b/solution.py
@@ -15,8 +15,9 @@
 HALF = RANK // 2
 FACTOR = 0.2 * (ROWS * COLS / RANK) ** 0.5
 
-GROUPS_X = [[x * Z + z for x in range(X)] for z in range(Z)]
-GROUPS_Z = [[x * Z + z for z in range(Z)] for x in range(X)]
+ROW_Y = [[2 * y + core for y in range(T // 2)] for core in range(2)]
+NEAR = [[x * Z + 2 * far + z for x in range(X) for z in range(2)] for far in range(Z // 2)]
+FAR = [[x * Z + 2 * far + z for far in range(Z // 2)] for x in range(X) for z in range(2)]
 
 
 def dot(left_side, right_side, left_dim, right_dim, precision=lax.Precision.HIGHEST):
@@ -41,6 +42,19 @@
 def gather(array, parts, axis, groups=None):
     blocks = exchange(jnp.broadcast_to(array, (parts, *array.shape)), axis, groups)
     return blocks.reshape(parts * array.shape[0], array.shape[1])
+
+
+def sum_over_tensor(part):
+    core = lax.axis_index("tensor") % 2
+    swap = [(t, t ^ 1) for t in range(T)]
+    mine = lax.dynamic_slice_in_dim(part, core * HALF, HALF, 0)
+    other = lax.dynamic_slice_in_dim(part, (1 - core) * HALF, HALF, 0)
+    mine = mine + lax.ppermute(other, "tensor", swap)
+    mine = gather(reduce_scatter(mine, T // 2, "tensor", ROW_Y), T // 2, "tensor", ROW_Y)
+    other = lax.ppermute(mine, "tensor", swap)
+    return jnp.where(
+        core == 0, jnp.concatenate([mine, other], axis=0), jnp.concatenate([other, mine], axis=0)
+    )
 
 
 def lane(group, k):
@@ -115,17 +129,17 @@
 
 def on_device(weights, momentum, gradient, right_factor):
     buffer = momentum + gradient.astype(jnp.float32)
-    part = dot(right_factor, buffer, 0, 1)
-    left_t = lax.all_gather(reduce_scatter(part, T, "tensor"), "tensor", tiled=True)
+    part = dot(right_factor, buffer, 0, 1, lax.Precision.HIGH)
+    left_t = sum_over_tensor(part)
     gram = dot(left_t, left_t, 1, 1)
-    raw = dot(buffer, left_t, 0, 1)
+    raw = dot(buffer, left_t, 0, 1, lax.Precision.HIGH)
     both = jnp.concatenate(
         [raw, jnp.concatenate([gram[:, :HALF], gram[:, HALF:]], axis=0)], axis=1
     )
-    both = reduce_scatter(both, X, "fsdp", GROUPS_X)
-    both = reduce_scatter(both, Z, "fsdp", GROUPS_Z)
-    both = gather(both, Z, "fsdp", GROUPS_Z)
-    both = gather(both, X, "fsdp", GROUPS_X)
+    both = reduce_scatter(both, len(FAR), "fsdp", NEAR)
+    both = reduce_scatter(both, len(NEAR), "fsdp", FAR)
+    both = gather(both, len(NEAR), "fsdp", FAR)
+    both = gather(both, len(FAR), "fsdp", NEAR)
     inverse, right, norms = factor(both)
     norms_sq = jnp.sum(exchange(jnp.broadcast_to(norms, (T, 1, RANK)), "tensor"), axis=0)
     basis_t = dot(inverse, left_t, 1, 0)

time: 159 us -> 152 us (0.956)
  blocking collectives: 119 us -> 94.3 us
  starting transfers between devices: 11.3 us -> 27.7 us
    ppermute x0 -> x2, starting transfers between devices: none -> 18.5 us  [the longest x1 16.1 us: sum_over_tensor(): mine = mine + lax.ppermute(other, 'tensor', swap)]
    all_gather x1 -> x0, blocking collectives: 16 us -> none  [on_device(): lax.all_gather(reduce_scatter(part, T, 'tensor'), 'tensor', tiled=True)]
    all_to_all x5 -> x6, blocking collectives: 103 us -> 94.3 us  [exchange(): return lax.all_to_all(blocks, axis, 0, 0, axis_index_groups=groups)]
    ppermute x0 -> x2, waiting for transfers between devices: none -> 2.18 us  [the longest x1 1.12 us: sum_over_tensor(): other = lax.ppermute(mine, 'tensor', swap)]
    all_to_all x1, starting transfers between devices: 11.3 us -> 9.14 us  [exchange(): return lax.all_to_all(blocks, axis, 0, 0, axis_index_groups=groups)]
  transfers between devices with their start and end apart: 1 -> 3, of which waited for: 1 -> 3; matrix products, arithmetic and copies ran while one was open for 1% -> 2% of each run, Pallas kernels for 0% -> 0%
where the time goes in v3:
time: 152 us; the launch traced here: 151 us
  blocking collectives  94.3 us (62%)
  starting transfers between devices  27.7 us (18%)
  Pallas kernels  10.3 us (7%)
  waiting for transfers between devices  7.1 us (5%)
  matrix products  6.86 us (5%)
  local copies, waits for them, and re-layouts  4.08 us (3%)
    all_to_all x6, blocking collectives, exchange(): return lax.all_to_all(blocks, axis, 0, 0, axis_index_groups=groups)  94.3 us
    ppermute x1, starting transfers between devices, sum_over_tensor(): mine = mine + lax.ppermute(other, 'tensor', swap)  16.1 us
    pallas_call x1, Pallas kernels, factor(): pl.pallas_call(factor_kernel, out_shape=(jax.ShapeDtypeStruct((RANK, RANK...  10.3 us
    all_to_all x1, starting transfers between devices, exchange(): return lax.all_to_all(blocks, axis, 0, 0, axis_index_groups=groups)  9.14 us
    dot_general x6, matrix products, dot(): lax.dot_general(left_side, right_side, (((left_dim,), (right_dim,)), ((),...  6.86 us
    all_to_all x1, waiting for transfers between devices, exchange(): return lax.all_to_all(blocks, axis, 0, 0, axis_index_groups=groups)  4.92 us
  transfers between devices with their start and end apart: 3, of which 3 were waited for; matrix products, arithmetic and copies ran while one was open for 2% of the time, Pallas kernels for 0%

profile of v3, /device:TPU:1, one launch (start us, length us, event | category | flops | bytes accessed | tf_op | source)
XLA Modules:
  0.0 151.4 jit_solution(364509469523435281)
XLA Ops:
  0.6 0.0 copy-start
  0.7 1.0 copy-done
  1.7 1.8 %fusion.4 = f32[416,256]{1,0:T(8,128)S(1)} fusion(f32[512,256]{1,0:T(8,128)S(1)} %copy-done, f32[416,512]{1,0:T(8,128)} %param.5, bf16[416,512]{1,0:T(8,128)(2,1)} %param.6), kind=kOutput, calls=%fused_computation.9 | convolution fusion | flops 327581696 | bytes 2228224 | tf_op jit(solution)/shard_map/dot_general | solution.py:24
  3.5 16.1 %collective-permute-start = (f32[128,416]{0,1:T(8,128)S(1)}, f32[128,416]{0,1:T(8,128)S(1)}, u32[]{:S(2)}, u32[]{:S(2)}) collective-permute-start(f32[128,416]{0,1:T(8,128)S(1)} %dynamic-slice_bitcast_fusion), channel_id=1, source_target_pairs={{0,1},{1,0},{2,3},{3,2},{4,5},{5,4},{6,7},{7,6},{8,9},{9,8},{10,11... | collective-permute-start | bytes 638984 | tf_op jit(solution)/shard_map/ppermute | solution.py:52
  19.6 1.1 collective-permute-done
  20.7 0.1 copy.17
  20.8 14.8 %all_to_all.35 = f32[8,16,416]{2,1,0:T(8,128)S(1)} all-to-all(f32[8,16,416]{2,1,0:T(8,128)S(1)} %bitcast.24), channel_id=1, replica_groups={{0,2,4,6,8,10,12,14},{1,3,5,7,9,11,13,15},{16,18,20,22,24,26,28,30},{17..., dimensions={0} | all-to-all | bytes 425984 | tf_op jit(solution)/shard_map/all_to_all | solution.py:34
  35.6 14.6 %all_to_all.36 = f32[8,16,416]{2,1,0:T(8,128)S(1)} all-to-all(f32[8,16,416]{2,1,0:T(8,128)S(1)} %broadcast_in_dim.12), channel_id=1, replica_groups={{0,2,4,6,8,10,12,14},{1,3,5,7,9,11,13,15},{16,18,20,22,24,26,28,30},{17..., dimensions={0} | all-to-all | bytes 425984 | tf_op jit(solution)/shard_map/all_to_all | solution.py:34
  50.3 0.0 copy-start.3
  50.3 2.5 %collective-permute-start.1 = (f32[128,416]{1,0:T(8,128)S(1)}, f32[128,416]{1,0:T(8,128)S(1)}, u32[]{:S(2)}, u32[]{:S(2)}) collective-permute-start(f32[128,416]{1,0:T(8,128)S(1)} %bitcast.20), channel_id=1, source_target_pairs={{0,1},{1,0},{2,3},{3,2},{4,5},{5,4},{6,7},{7,6},{8,9},{9,8},{10,11... | collective-permute-start | bytes 638984 | tf_op jit(solution)/shard_map/ppermute | solution.py:54
  52.8 0.0 copy-start.1
  52.8 1.1 collective-permute-done.1
  53.9 0.0 copy-start.6
  53.9 0.6 fusion.6
  54.5 0.0 copy-start.2
  54.6 0.0 copy-done.3
  54.6 0.0 copy-done.6
  54.6 0.0 copy-done.1
  54.6 0.9 copy-done.2
  55.6 0.6 fusion.3
  56.2 0.1 maximum_maximum_fusion
  56.3 0.3 copy.20
  56.6 15.1 %all_to_all.37 = f32[8,64,384]{2,1,0:T(8,128)S(1)} all-to-all(f32[8,64,384]{2,1,0:T(8,128)S(1)} %bitcast.19), channel_id=1, replica_groups={{0,16,256,272,512,528,768,784},{32,48,288,304,544,560,800,816},{64,80,3..., dimensions={0} | all-to-all | bytes 1572864 | tf_op jit(solution)/shard_map/all_to_all | solution.py:34
  71.7 23.2 %all_to_all.38 = f32[8,8,384]{2,1,0:T(8,128)S(1)} all-to-all(f32[8,8,384]{2,1,0:T(8,128)S(1)} %bitcast.25), channel_id=1, replica_groups={{0,32,64,96,128,160,192,224},{16,48,80,112,144,176,208,240},{256,288,32..., dimensions={0} | all-to-all | bytes 196608 | tf_op jit(solution)/shard_map/all_to_all | solution.py:34
  94.9 14.9 %all_to_all.39 = f32[8,8,384]{2,1,0:T(8,128)S(1)} all-to-all(f32[8,8,384]{2,1,0:T(8,128)S(1)} %broadcast_in_dim.13), channel_id=1, replica_groups={{0,32,64,96,128,160,192,224},{16,48,80,112,144,176,208,240},{256,288,32..., dimensions={0} | all-to-all | bytes 196608 | tf_op jit(solution)/shard_map/all_to_all | solution.py:34
  109.8 0.1 broadcast_in_dim.14
  109.9 11.7 %all_to_all.40 = f32[8,64,384]{2,1,0:T(8,128)S(1)} all-to-all(f32[8,64,384]{2,1,0:T(8,128)S(1)} %broadcast_in_dim.14), channel_id=1, replica_groups={{0,16,256,272,512,528,768,784},{32,48,288,304,544,560,800,816},{64,80,3..., dimensions={0} | all-to-all | bytes 1572864 | tf_op jit(solution)/shard_map/all_to_all | solution.py:34
  121.6 0.0 copy-start.4
  121.6 0.0 copy-start.7
  121.6 10.3 %shard_map.67 = (f32[256,256]{1,0:T(8,128)S(1)}, f32[512,256]{1,0:T(8,128)S(1)}, f32[1,256]{1,0:T(1,128)S(1)}) custom-call(f32[512,384]{1,0:T(8,128)S(1)} %bitcast.17), custom_call_target="tpu_custom_call" | custom-call | flops 1000000000 | bytes 2000000 | tf_op jit(solution)/shard_map/pallas_call | solution.py:115
  131.9 0.6 broadcast_in_dim.15
  132.5 9.1 %all-to-all-start.6 = ((f32[16,1,256]{2,1,0:T(1,128)}), f32[16,1,256]{2,1,0:T(1,128)S(1)}, u32[]{:S(2)}, u32[]{:S(2)}) async-start(f32[16,1,256]{2,1,0:T(1,128)} %broadcast_in_dim.15), calls=%async_computation.6 | async-start | bytes 32768 | tf_op jit(solution)/shard_map/all_to_all | solution.py:34
  141.6 0.0 copy-done.4
  141.6 0.0 copy-done.7
  141.6 1.0 fusion.5
  142.6 1.5 fusion
  144.1 4.9 %all-to-all-done.6 = f32[16,1,256]{2,1,0:T(1,128)S(1)} async-done(((f32[16,1,256]{2,1,0:T(1,128)}), f32[16,1,256]{2,1,0:T(1,128)S(1)}, u32[]{:S(2)}, u32[]{:S(2)}) %all-to-all-start.6) | async-done | bytes 16416 | tf_op jit(solution)/shard_map/all_to_all | solution.py:34
  149.1 0.0 copy-start.8
  149.1 1.0 copy-done.8
  150.1 0.0 copy-start.5
  150.1 1.3 fusion.2
  151.4 0.0 copy-done.5
  (11 shorter events, 0.3 us)
Async XLA Ops:
  0.6 1.0 copy-start
  3.5 17.1 %collective-permute-start = (f32[128,416]{0,1:T(8,128)S(1)}, f32[128,416]{0,1:T(8,128)S(1)}, u32[]{:S(2)}, u32[]{:S(2)}) collective-permute-start(f32[128,416]{0,1:T(8,128)S(1)} %dynamic-slice_bitcast_fusion), channel_id=1, source_target_pairs={{0,1},{1,0},{2,3},{3,2},{4,5},{5,4},{6,7},{7,6},{8,9},{9,8},{10,11... | collective-permute-start | bytes 638984 | tf_op jit(solution)/shard_map/ppermute | solution.py:52
  50.3 4.3 %copy-start.3 = (f32[8,16,416]{2,1,0:T(8,128)}, f32[8,16,416]{2,1,0:T(8,128)S(1)}, u32[]{:S(2)}) copy-start(f32[8,16,416]{2,1,0:T(8,128)S(1)} %all_to_all.36) | copy-start | bytes 638980
  50.3 3.6 %collective-permute-start.1 = (f32[128,416]{1,0:T(8,128)S(1)}, f32[128,416]{1,0:T(8,128)S(1)}, u32[]{:S(2)}, u32[]{:S(2)}) collective-permute-start(f32[128,416]{1,0:T(8,128)S(1)} %bitcast.20), channel_id=1, source_target_pairs={{0,1},{1,0},{2,3},{3,2},{4,5},{5,4},{6,7},{7,6},{8,9},{9,8},{10,11... | collective-permute-start | bytes 638984 | tf_op jit(solution)/shard_map/ppermute | solution.py:54
  52.8 1.8 %copy-start.1 = (f32[416,512]{1,0:T(8,128)S(1)}, f32[416,512]{1,0:T(8,128)}, u32[]{:S(2)}) copy-start(f32[416,512]{1,0:T(8,128)} %param.5) | copy-start | bytes 2555908
  53.9 0.7 copy-start.6
  54.5 1.0 copy-start.2
  121.6 20.0 %copy-start.4 = (f32[8,16,416]{2,1,0:T(8,128)S(1)}, f32[8,16,416]{2,1,0:T(8,128)}, u32[]{:S(2)}) copy-start(f32[8,16,416]{2,1,0:T(8,128)} %copy-done.3) | copy-start | bytes 638980
  121.6 20.0 %copy-start.7 = (f32[128,416]{1,0:T(8,128)S(1)}, f32[128,416]{1,0:T(8,128)}, u32[]{:S(2)}) copy-start(f32[128,416]{1,0:T(8,128)} %copy-done.6) | copy-start | bytes 638980
  132.5 16.6 %all-to-all-start.6 = ((f32[16,1,256]{2,1,0:T(1,128)}), f32[16,1,256]{2,1,0:T(1,128)S(1)}, u32[]{:S(2)}, u32[]{:S(2)}) async-start(f32[16,1,256]{2,1,0:T(1,128)} %broadcast_in_dim.15), calls=%async_computation.6 | async-start | bytes 32768 | tf_op jit(solution)/shard_map/all_to_all | solution.py:34
  149.1 1.0 copy-start.8
  150.1 1.3 copy-start.5

commit v4 on v3

--- a/solution.py
+++ b/solution.py
@@ -11,7 +11,7 @@
 X = 4
 Z = 16
 T = 16
-BLOCK = 64
+BLOCK = 128
 HALF = RANK // 2
 FACTOR = 0.2 * (ROWS * COLS / RANK) ** 0.5
 
@@ -30,6 +30,30 @@
     )
 
 
+def dot3(left_side, right_side, left_dim, right_dim):
+    left_high = left_side.astype(jnp.bfloat16)
+    right_high = right_side.astype(jnp.bfloat16)
+    left_low = (left_side - left_high.astype(jnp.float32)).astype(jnp.bfloat16)
+    right_low = (right_side - right_high.astype(jnp.float32)).astype(jnp.bfloat16)
+    dims = (left_dim, right_dim, lax.Precision.DEFAULT)
+    small = dot(left_high, right_low, *dims) + dot(left_low, right_high, *dims)
+    return small + dot(left_high, right_high, *dims)
+
+
+def local_kernel(body, out_shape, *args, scalars=0, scratch=(), space=pltpu.VMEM, limit=24):
+    places = [pl.BlockSpec(memory_space=pltpu.SMEM)] * scalars
+    places += [pl.BlockSpec(memory_space=space)] * (len(args) - scalars)
+    return pl.pallas_call(
+        body,
+        out_shape=[jax.ShapeDtypeStruct(shape, kind) for shape, kind in out_shape],
+        in_specs=places,
+        out_specs=[pl.BlockSpec(memory_space=pltpu.VMEM)] * len(out_shape),
+        scratch_shapes=scratch,
+        compiler_params=pltpu.CompilerParams(vmem_limit_bytes=limit * 2**20),
+        cost_estimate=pl.CostEstimate(flops=10**9, bytes_accessed=2 * 10**6, transcendentals=0),
+    )(*args)
+
+
 def exchange(blocks, axis, groups=None):
     return lax.all_to_all(blocks, axis, 0, 0, axis_index_groups=groups)
 
@@ -44,17 +68,88 @@
     return blocks.reshape(parts * array.shape[0], array.shape[1])
 
 
-def sum_over_tensor(part):
-    core = lax.axis_index("tensor") % 2
+def sum_over_tensor(mine, other):
     swap = [(t, t ^ 1) for t in range(T)]
-    mine = lax.dynamic_slice_in_dim(part, core * HALF, HALF, 0)
-    other = lax.dynamic_slice_in_dim(part, (1 - core) * HALF, HALF, 0)
     mine = mine + lax.ppermute(other, "tensor", swap)
-    mine = gather(reduce_scatter(mine, T // 2, "tensor", ROW_Y), T // 2, "tensor", ROW_Y)
-    other = lax.ppermute(mine, "tensor", swap)
-    return jnp.where(
-        core == 0, jnp.concatenate([mine, other], axis=0), jnp.concatenate([other, mine], axis=0)
-    )
+    mine = jnp.sum(exchange(mine, "tensor", ROW_Y), axis=0)
+    mine = exchange(jnp.broadcast_to(mine, other.shape), "tensor", ROW_Y)
+    return mine, lax.ppermute(mine, "tensor", swap)
+
+
+def start_kernel(
+    core, momentum, gradient, right_factor, mine, other, held, grad, factor, left, sems
+):
+    rows = momentum.shape[0]
+    parts = [pl.ds(start, rows // 2) for start in (0, rows // 2)]
+    first = pltpu.make_async_copy(right_factor, factor, sems.at[0])
+    loads = [
+        (
+            pltpu.make_async_copy(momentum.at[part], held.at[part], sems.at[1 + 2 * i]),
+            pltpu.make_async_copy(gradient.at[part], grad.at[part], sems.at[2 + 2 * i]),
+        )
+        for i, part in enumerate(parts)
+    ]
+    first.start()
+    for load in loads:
+        load[0].start()
+        load[1].start()
+    first.wait()
+    for part, load in zip(parts, loads):
+        load[0].wait()
+        load[1].wait()
+        total = held[part, :] + grad[part, :].astype(jnp.float32)
+        left[part, :] = dot3(total, factor[...], 1, 0)
+    step = rows // (T // 2)
+
+    @pl.when(core[0] == 0)
+    def _():
+        for i in range(T // 2):
+            mine[i] = left[step * i : step * (i + 1), :HALF]
+            other[i] = left[step * i : step * (i + 1), HALF:]
+
+    @pl.when(core[0] == 1)
+    def _():
+        for i in range(T // 2):
+            mine[i] = left[step * i : step * (i + 1), HALF:]
+            other[i] = left[step * i : step * (i + 1), :HALF]
+
+
+def products_kernel(core, mine, other, momentum, gradient, left_t, both):
+    mine_t = jnp.concatenate([mine[i] for i in range(T // 2)], axis=0).T
+    other_t = jnp.concatenate([other[i] for i in range(T // 2)], axis=0).T
+
+    @pl.when(core[0] == 0)
+    def _():
+        left_t[:HALF] = mine_t
+        left_t[HALF:] = other_t
+
+    @pl.when(core[0] == 1)
+    def _():
+        left_t[HALF:] = mine_t
+        left_t[:HALF] = other_t
+
+    buffer = momentum[...] + gradient[...].astype(jnp.float32)
+    left = left_t[...]
+    gram = dot(left, left, 1, 1)
+    both[:RANK, RANK:] = gram[:, :HALF]
+    both[RANK:, RANK:] = gram[:, HALF:]
+    raw = dot3(left, buffer, 1, 0)
+    both[:RANK, :RANK] = raw[:, :RANK]
+    both[RANK:, :RANK] = raw[:, RANK:]
+
+
+def momentum_kernel(inverse, left_t, right_t, momentum, gradient, basis, right, new_momentum):
+    basis[...] = dot3(inverse[...], left_t[...], 1, 0).T
+    right[...] = right_t[...].T
+    buffer = momentum[...] + gradient[...].astype(jnp.float32)
+    new_momentum[...] = buffer - 0.05 * dot3(basis[...], right_t[...], 1, 0)
+
+
+def weights_kernel(norms, basis, right_t, right, weights, new_weights, new_right):
+    scale = 1.0 / (jnp.sqrt(jnp.sum(norms[...], axis=0)) + 1e-06)
+    new_right[...] = right[...] * scale
+    step = dot3(basis[...] * (FACTOR * scale), right_t[...], 1, 0)
+    new_weights[...] = (weights[...].astype(jnp.float32) - step).astype(jnp.bfloat16)
 
 
 def lane(group, k):
@@ -105,48 +200,59 @@
         inverse_ref[start:stop, :] = block[:, RANK:]
         if stop < RANK:
             work[stop:, :] = work[stop:, :] - dot(block[:, :RANK].T[stop:, :], block, 1, 0)
-    right = dot(both_ref[:, :RANK], inverse_ref[...], 1, 1)
-    right_ref[...] = right
-    norms_ref[...] = jnp.sum(right * right, axis=0, keepdims=True)
-
-
-def factor(both):
-    cols = both.shape[0]
-    return pl.pallas_call(
-        factor_kernel,
-        out_shape=(
-            jax.ShapeDtypeStruct((RANK, RANK), jnp.float32),
-            jax.ShapeDtypeStruct((cols, RANK), jnp.float32),
-            jax.ShapeDtypeStruct((1, RANK), jnp.float32),
-        ),
-        in_specs=[pl.BlockSpec(memory_space=pltpu.VMEM)],
-        out_specs=[pl.BlockSpec(memory_space=pltpu.VMEM)] * 3,
-        scratch_shapes=[pltpu.VMEM((RANK, 2 * RANK), jnp.float32)],
-        compiler_params=pltpu.CompilerParams(vmem_limit_bytes=24 * 2**20),
-        cost_estimate=pl.CostEstimate(flops=10**9, bytes_accessed=2 * 10**6, transcendentals=0),
-    )(both)
+    inverse = inverse_ref[...]
+    squares = jnp.zeros((RANK, HALF), jnp.float32)
+    for half in range(2):
+        right = dot3(inverse, both_ref[half * RANK : (half + 1) * RANK, :RANK], 1, 0)
+        right_ref[:, half * RANK : (half + 1) * RANK] = right
+        squares = squares + right[:, :HALF] * right[:, :HALF] + right[:, HALF:] * right[:, HALF:]
+    norms = dot(jnp.ones((8, HALF), jnp.float32), squares, 1, 1)
+    norms_ref[...] = jnp.broadcast_to(norms[:1].reshape(1, 1, RANK), norms_ref.shape)
 
 
 def on_device(weights, momentum, gradient, right_factor):
-    buffer = momentum + gradient.astype(jnp.float32)
-    part = dot(right_factor, buffer, 0, 1, lax.Precision.HIGH)
-    left_t = sum_over_tensor(part)
-    gram = dot(left_t, left_t, 1, 1)
-    raw = dot(buffer, left_t, 0, 1, lax.Precision.HIGH)
-    both = jnp.concatenate(
-        [raw, jnp.concatenate([gram[:, :HALF], gram[:, HALF:]], axis=0)], axis=1
+    rows, cols = momentum.shape
+    wide = jnp.float32
+    blocks = (T // 2, rows // (T // 2), HALF)
+    core = (lax.axis_index("tensor") % 2).reshape(1)
+    mine, other = local_kernel(
+        start_kernel,
+        [(blocks, wide), (blocks, wide)],
+        core, momentum, gradient, right_factor, scalars=1, space=pltpu.HBM, limit=56,
+        scratch=[
+            pltpu.VMEM((rows, cols), wide),
+            pltpu.VMEM((rows, cols), jnp.bfloat16),
+            pltpu.VMEM((cols, RANK), wide),
+            pltpu.VMEM((rows, RANK), wide),
+            pltpu.SemaphoreType.DMA((5,)),
+        ],
+    )
+    mine, other = sum_over_tensor(mine, other)
+    left_t, both = local_kernel(
+        products_kernel,
+        [((RANK, rows), wide), ((2 * RANK, RANK + HALF), wide)],
+        core, mine, other, momentum, gradient, scalars=1,
     )
     both = reduce_scatter(both, len(FAR), "fsdp", NEAR)
     both = reduce_scatter(both, len(NEAR), "fsdp", FAR)
     both = gather(both, len(NEAR), "fsdp", FAR)
     both = gather(both, len(FAR), "fsdp", NEAR)
-    inverse, right, norms = factor(both)
-    norms_sq = jnp.sum(exchange(jnp.broadcast_to(norms, (T, 1, RANK)), "tensor"), axis=0)
-    basis_t = dot(inverse, left_t, 1, 0)
-    new_right = right / (jnp.sqrt(norms_sq) + 1e-06)
-    new_momentum = buffer - 0.05 * dot(basis_t, right, 0, 1, lax.Precision.HIGH)
-    new_weights = (weights.astype(jnp.float32) - FACTOR * dot(basis_t, new_right, 0, 1, lax.Precision.HIGH)).astype(
-        jnp.bfloat16
+    inverse, right_t, norms = local_kernel(
+        factor_kernel,
+        [((RANK, RANK), wide), ((RANK, cols), wide), ((T, 1, RANK), wide)],
+        both,
+        scratch=[pltpu.VMEM((RANK, 2 * RANK), jnp.float32)],
+    )
+    norms = exchange(norms, "tensor")
+    basis, right, new_momentum = local_kernel(
+        momentum_kernel,
+        [((rows, RANK), wide), ((cols, RANK), wide), ((rows, cols), wide)],
+        inverse, left_t, right_t, momentum, gradient,
+    )
+    new_weights, new_right = local_kernel(
+        weights_kernel,
+        [((rows, cols), jnp.bfloat16), ((cols, RANK), wide)],
+        norms, basis, right_t, right, weights,
     )
     return (new_weights, new_momentum, new_right)
 

time: 152 us -> 150 us (0.987)
  Pallas kernels: 10.3 us -> 17.9 us
  matrix products: 6.86 us -> 0 us
  blocking collectives: 94.3 us -> 91.9 us
  local copies, waits for them, and re-layouts: 4.08 us -> 1.85 us
    pallas_call x1 -> x5, Pallas kernels: 10.3 us -> 17.9 us  [local_kernel(): pl.pallas_call(body, out_shape=[jax.ShapeDtypeStruct(shape, kind) for sha...]
    dot_general x6 -> x0, matrix products: 6.86 us -> none  [dot(): lax.dot_general(left_side, right_side, (((left_dim,), (right_dim,)), ((),...]
    all_to_all x6, blocking collectives: 94.3 us -> 91.9 us  [exchange(): return lax.all_to_all(blocks, axis, 0, 0, axis_index_groups=groups)]
  transfers between devices with their start and end apart: 3 -> 3, of which waited for: 3 -> 3; matrix products, arithmetic and copies ran while one was open for 2% -> 0% of each run, Pallas kernels for 0% -> 1%
where the time goes in v4:
time: 150 us; the launch traced here: 149 us
  blocking collectives  91.9 us (61%)
  starting transfers between devices  28.8 us (19%)
  Pallas kernels  17.9 us (12%)
  waiting for transfers between devices  7.24 us (5%)
  local copies, waits for them, and re-layouts  1.85 us (1%)
    all_to_all x6, blocking collectives, exchange(): return lax.all_to_all(blocks, axis, 0, 0, axis_index_groups=groups)  91.9 us
    pallas_call x5, Pallas kernels, local_kernel(): pl.pallas_call(body, out_shape=[jax.ShapeDtypeStruct(shape, kind) for sha...  17.9 us
    ppermute x1, starting transfers between devices, sum_over_tensor(): mine = mine + lax.ppermute(other, 'tensor', swap)  16.1 us
    all_to_all x1, starting transfers between devices, exchange(): return lax.all_to_all(blocks, axis, 0, 0, axis_index_groups=groups)  9.15 us
    all_to_all x1, waiting for transfers between devices, exchange(): return lax.all_to_all(blocks, axis, 0, 0, axis_index_groups=groups)  4.85 us
    ppermute x1, starting transfers between devices, sum_over_tensor(): return (mine, lax.ppermute(mine, 'tensor', swap))  3.61 us
  transfers between devices with their start and end apart: 3, of which 3 were waited for; matrix products, arithmetic and copies ran while one was open for 0% of the time, Pallas kernels for 1%

profile of v4, /device:TPU:1, one launch (start us, length us, event | category | flops | bytes accessed | tf_op | source)
XLA Modules:
  0.0 149.4 jit_solution(10215839421469071075)
XLA Ops:
  0.6 3.0 %shard_map.67 = (f32[8,52,128]{2,1,0:T(8,128)}, f32[8,52,128]{2,1,0:T(8,128)}) custom-call(s32[1]{0:T(128)} %bitcast.core, f32[416,512]{1,0:T(8,128)} %momentum.5, bf16[416,512]{1,0:T(8,128)(2,1)} %gradient.5, f32[512,256]{1,0:T(8,128)} %right_factor.1), custom_call_target="tpu_custom_call" | custom-call | flops 1000000000 | bytes 2000000 | tf_op jit(solution)/shard_map/pallas_call | solution.py:46
  3.7 16.1 %collective-permute-start = (f32[8,52,128]{2,1,0:T(8,128)}, f32[8,52,128]{2,1,0:T(8,128)S(1)}, u32[]{:S(2)}, u32[]{:S(2)}) collective-permute-start(f32[8,52,128]{2,1,0:T(8,128)} %get-tuple-element.16), channel_id=1, source_target_pairs={{0,1},{1,0},{2,3},{3,2},{4,5},{5,4},{6,7},{7,6},{8,9},{9,8},{10,11... | collective-permute-start | bytes 638984 | tf_op jit(solution)/shard_map/ppermute | solution.py:73
  19.7 1.3 collective-permute-done
  21.0 1.0 add.8
  22.0 0.0 copy-start
  22.0 14.1 %all_to_all.35 = f32[8,52,128]{2,1,0:T(8,128)S(1)} all-to-all(f32[8,52,128]{2,1,0:T(8,128)S(1)} %add.8), channel_id=1, replica_groups={{0,2,4,6,8,10,12,14},{1,3,5,7,9,11,13,15},{16,18,20,22,24,26,28,30},{17..., dimensions={0} | all-to-all | bytes 425984 | tf_op jit(solution)/shard_map/all_to_all | solution.py:58
  36.1 0.0 copy-start.1
  36.2 12.9 %all_to_all.36.mine = f32[8,52,128]{2,1,0:T(8,128)S(1)} all-to-all(f32[8,52,128]{2,1,0:T(8,128)S(1)} %broadcast_in_dim.9), channel_id=1, replica_groups={{0,2,4,6,8,10,12,14},{1,3,5,7,9,11,13,15},{16,18,20,22,24,26,28,30},{17..., dimensions={0} | all-to-all | bytes 425984 | tf_op jit(solution)/shard_map/all_to_all | solution.py:58
  49.1 3.6 %collective-permute-start.1 = (f32[8,52,128]{2,1,0:T(8,128)S(1)}, f32[8,52,128]{2,1,0:T(8,128)S(1)}, u32[]{:S(2)}, u32[]{:S(2)}) collective-permute-start(f32[8,52,128]{2,1,0:T(8,128)S(1)} %all_to_all.36.mine), channel_id=1, source_target_pairs={{0,1},{1,0},{2,3},{3,2},{4,5},{5,4},{6,7},{7,6},{8,9},{9,8},{10,11... | collective-permute-start | bytes 638984 | tf_op jit(solution)/shard_map/ppermute | solution.py:76
  52.7 1.1 collective-permute-done.1.other
  53.8 0.0 copy-done
  53.8 0.0 copy-done.1
  53.8 1.3 shard_map.68
  55.1 15.1 %all_to_all.37 = f32[8,64,384]{2,1,0:T(8,128)S(1)} all-to-all(f32[8,64,384]{2,1,0:T(8,128)S(1)} %bitcast.5), channel_id=1, replica_groups={{0,16,256,272,512,528,768,784},{32,48,288,304,544,560,800,816},{64,80,3..., dimensions={0} | all-to-all | bytes 1572864 | tf_op jit(solution)/shard_map/all_to_all | solution.py:58
  70.2 23.1 %all_to_all.38 = f32[8,8,384]{2,1,0:T(8,128)S(1)} all-to-all(f32[8,8,384]{2,1,0:T(8,128)S(1)} %bitcast.7), channel_id=1, replica_groups={{0,32,64,96,128,160,192,224},{16,48,80,112,144,176,208,240},{256,288,32..., dimensions={0} | all-to-all | bytes 196608 | tf_op jit(solution)/shard_map/all_to_all | solution.py:58
  93.4 14.9 %all_to_all.39 = f32[8,8,384]{2,1,0:T(8,128)S(1)} all-to-all(f32[8,8,384]{2,1,0:T(8,128)S(1)} %broadcast_in_dim.10), channel_id=1, replica_groups={{0,32,64,96,128,160,192,224},{16,48,80,112,144,176,208,240},{256,288,32..., dimensions={0} | all-to-all | bytes 196608 | tf_op jit(solution)/shard_map/all_to_all | solution.py:58
  108.3 0.1 broadcast_in_dim.11
  108.3 11.7 %all_to_all.40 = f32[8,64,384]{2,1,0:T(8,128)S(1)} all-to-all(f32[8,64,384]{2,1,0:T(8,128)S(1)} %broadcast_in_dim.11), channel_id=1, replica_groups={{0,16,256,272,512,528,768,784},{32,48,288,304,544,560,800,816},{64,80,3..., dimensions={0} | all-to-all | bytes 1572864 | tf_op jit(solution)/shard_map/all_to_all | solution.py:58
  120.1 10.4 %shard_map.69 = (f32[256,256]{1,0:T(8,128)S(1)}, f32[256,512]{1,0:T(8,128)S(1)}, f32[16,1,256]{2,1,0:T(1,128)}) custom-call(f32[512,384]{1,0:T(8,128)S(1)} %bitcast.6), custom_call_target="tpu_custom_call" | custom-call | flops 1000000000 | bytes 2000000 | tf_op jit(solution)/shard_map/pallas_call | solution.py:46
  130.4 9.1 %all-to-all-start.6 = ((f32[16,1,256]{2,1,0:T(1,128)}), f32[16,1,256]{2,1,0:T(1,128)S(1)}, u32[]{:S(2)}, u32[]{:S(2)}) async-start(f32[16,1,256]{2,1,0:T(1,128)} %get-tuple-element.18), calls=%async_computation.6 | async-start | bytes 32768 | tf_op jit(solution)/shard_map/all_to_all | solution.py:58
  139.6 0.0 copy-start.2
  139.6 1.8 %shard_map.70 = (f32[416,256]{1,0:T(8,128)S(1)}, f32[512,256]{1,0:T(8,128)S(1)}, f32[416,512]{1,0:T(8,128)}) custom-call(f32[256,256]{1,0:T(8,128)S(1)} %get-tuple-element.19.inverse, f32[256,416]{1,0:T(8,128)S(1)} %get-tuple-element.20.left_t, f32[256,512]{1,0:T(8,128)S(1)} %get-tuple-element.21.right_t, f32[416,512]{1,0:T(8,128)S(1)} %copy-done, ...), custom_call_target="tpu_custom_call" | custom-call | flops 1000000000 | bytes 2000000 | tf_op jit(solution)/shard_map/pallas_call | solution.py:46
  141.4 0.0 copy-start.3
  141.4 0.8 copy-done.3
  142.1 4.8 %all-to-all-done.6.norms = f32[16,1,256]{2,1,0:T(1,128)S(1)} async-done(((f32[16,1,256]{2,1,0:T(1,128)}), f32[16,1,256]{2,1,0:T(1,128)S(1)}, u32[]{:S(2)}, u32[]{:S(2)}) %all-to-all-start.6) | async-done | bytes 16416 | tf_op jit(solution)/shard_map/all_to_all | solution.py:58
  147.0 0.0 copy-done.2
  147.0 0.0 copy-start.4
  147.0 1.0 copy-done.4
  148.0 1.4 shard_map.71
  (5 shorter events, 0.1 us)
Async XLA Ops:
  3.7 17.4 %collective-permute-start = (f32[8,52,128]{2,1,0:T(8,128)}, f32[8,52,128]{2,1,0:T(8,128)S(1)}, u32[]{:S(2)}, u32[]{:S(2)}) collective-permute-start(f32[8,52,128]{2,1,0:T(8,128)} %get-tuple-element.16), channel_id=1, source_target_pairs={{0,1},{1,0},{2,3},{3,2},{4,5},{5,4},{6,7},{7,6},{8,9},{9,8},{10,11... | collective-permute-start | bytes 638984 | tf_op jit(solution)/shard_map/ppermute | solution.py:73
  22.0 31.8 %copy-start = (f32[416,512]{1,0:T(8,128)S(1)}, f32[416,512]{1,0:T(8,128)}, u32[]{:S(2)}) copy-start(f32[416,512]{1,0:T(8,128)} %momentum.5) | copy-start | bytes 2555908
  36.1 17.7 %copy-start.1 = (bf16[416,512]{1,0:T(8,128)(2,1)S(1)}, bf16[416,512]{1,0:T(8,128)(2,1)}, u32[]{:S(2)}) copy-start(bf16[416,512]{1,0:T(8,128)(2,1)} %gradient.5) | copy-start | bytes 1277956
  49.1 4.7 %collective-permute-start.1 = (f32[8,52,128]{2,1,0:T(8,128)S(1)}, f32[8,52,128]{2,1,0:T(8,128)S(1)}, u32[]{:S(2)}, u32[]{:S(2)}) collective-permute-start(f32[8,52,128]{2,1,0:T(8,128)S(1)} %all_to_all.36.mine), channel_id=1, source_target_pairs={{0,1},{1,0},{2,3},{3,2},{4,5},{5,4},{6,7},{7,6},{8,9},{9,8},{10,11... | collective-permute-start | bytes 638984 | tf_op jit(solution)/shard_map/ppermute | solution.py:76
  130.4 16.6 %all-to-all-start.6 = ((f32[16,1,256]{2,1,0:T(1,128)}), f32[16,1,256]{2,1,0:T(1,128)S(1)}, u32[]{:S(2)}, u32[]{:S(2)}) async-start(f32[16,1,256]{2,1,0:T(1,128)} %get-tuple-element.18), calls=%async_computation.6 | async-start | bytes 32768 | tf_op jit(solution)/shard_map/all_to_all | solution.py:58
  139.6 7.4 %copy-start.2 = (bf16[416,512]{1,0:T(8,128)(2,1)S(1)}, bf16[416,512]{1,0:T(8,128)(2,1)}, u32[]{:S(2)}) copy-start(bf16[416,512]{1,0:T(8,128)(2,1)} %weights.1) | copy-start | bytes 1277956
  141.4 0.8 copy-start.3
  147.0 1.0 copy-start.4

commit v5 on v4

--- a/solution.py
+++ b/solution.py
@@ -138,17 +138,18 @@
     both[RANK:, :RANK] = raw[:, RANK:]
 
 
-def momentum_kernel(inverse, left_t, right_t, momentum, gradient, basis, right, new_momentum):
-    basis[...] = dot3(inverse[...], left_t[...], 1, 0).T
+def momentum_kernel(inverse, left_t, right_t, momentum, gradient, right, new_momentum):
+    basis = dot3(inverse[...], left_t[...], 1, 0).T
     right[...] = right_t[...].T
     buffer = momentum[...] + gradient[...].astype(jnp.float32)
-    new_momentum[...] = buffer - 0.05 * dot3(basis[...], right_t[...], 1, 0)
-
-
-def weights_kernel(norms, basis, right_t, right, weights, new_weights, new_right):
+    new_momentum[...] = buffer - 0.05 * dot3(basis, right_t[...], 1, 0)
+
+
+def weights_kernel(norms, inverse, left_t, right_t, right, weights, new_weights, new_right):
     scale = 1.0 / (jnp.sqrt(jnp.sum(norms[...], axis=0)) + 1e-06)
     new_right[...] = right[...] * scale
-    step = dot3(basis[...] * (FACTOR * scale), right_t[...], 1, 0)
+    basis = dot3(inverse[...], left_t[...], 1, 0).T
+    step = dot3(basis * (FACTOR * scale), right_t[...], 1, 0)
     new_weights[...] = (weights[...].astype(jnp.float32) - step).astype(jnp.bfloat16)
 
 
@@ -244,15 +245,15 @@
         scratch=[pltpu.VMEM((RANK, 2 * RANK), jnp.float32)],
     )
     norms = exchange(norms, "tensor")
-    basis, right, new_momentum = local_kernel(
+    right, new_momentum = local_kernel(
         momentum_kernel,
-        [((rows, RANK), wide), ((cols, RANK), wide), ((rows, cols), wide)],
+        [((cols, RANK), wide), ((rows, cols), wide)],
         inverse, left_t, right_t, momentum, gradient,
     )
     new_weights, new_right = local_kernel(
         weights_kernel,
         [((rows, cols), jnp.bfloat16), ((cols, RANK), wide)],
-        norms, basis, right_t, right, weights,
+        norms, inverse, left_t, right_t, right, weights,
     )
     return (new_weights, new_momentum, new_right)
 

time: 150 us -> 149 us (level)
  local copies, waits for them, and re-layouts: 1.85 us -> 0.09 us
    unnamed x10 -> x6, local copies, waits for them, and re-layouts: 1.78 us -> 0.01 us
where the time goes in v5:
time: 149 us
  blocking collectives  91.9 us (62%)
  starting transfers between devices  28.8 us (19%)
  Pallas kernels  18.3 us (12%)
  waiting for transfers between devices  7.99 us (5%)
    all_to_all x6, blocking collectives, exchange(): return lax.all_to_all(blocks, axis, 0, 0, axis_index_groups=groups)  91.9 us
    pallas_call x5, Pallas kernels, local_kernel(): pl.pallas_call(body, out_shape=[jax.ShapeDtypeStruct(shape, kind) for sha...  18.3 us
    ppermute x1, starting transfers between devices, sum_over_tensor(): mine = mine + lax.ppermute(other, 'tensor', swap)  16.1 us
    all_to_all x1, starting transfers between devices, exchange(): return lax.all_to_all(blocks, axis, 0, 0, axis_index_groups=groups)  9.15 us
    all_to_all x1, waiting for transfers between devices, exchange(): return lax.all_to_all(blocks, axis, 0, 0, axis_index_groups=groups)  5.59 us
    ppermute x1, starting transfers between devices, sum_over_tensor(): return (mine, lax.ppermute(mine, 'tensor', swap))  3.61 us
  transfers between devices with their start and end apart: 3, of which 3 were waited for; matrix products, arithmetic and copies ran while one was open for 0% of the time, Pallas kernels for 1%

profile of v5, /device:TPU:1, one launch (start us, length us, event | category | flops | bytes accessed | tf_op | source)
XLA Modules:
  0.0 148.8 jit_solution(597141701863504079)
XLA Ops:
  0.6 3.0 %shard_map.67 = (f32[8,52,128]{2,1,0:T(8,128)}, f32[8,52,128]{2,1,0:T(8,128)}) custom-call(s32[1]{0:T(128)} %bitcast.core, f32[416,512]{1,0:T(8,128)} %momentum.5, bf16[416,512]{1,0:T(8,128)(2,1)} %gradient.5, f32[512,256]{1,0:T(8,128)} %right_factor.1), custom_call_target="tpu_custom_call" | custom-call | flops 1000000000 | bytes 2000000 | tf_op jit(solution)/shard_map/pallas_call | solution.py:46
  3.7 16.1 %collective-permute-start = (f32[8,52,128]{2,1,0:T(8,128)}, f32[8,52,128]{2,1,0:T(8,128)S(1)}, u32[]{:S(2)}, u32[]{:S(2)}) collective-permute-start(f32[8,52,128]{2,1,0:T(8,128)} %get-tuple-element.15), channel_id=1, source_target_pairs={{0,1},{1,0},{2,3},{3,2},{4,5},{5,4},{6,7},{7,6},{8,9},{9,8},{10,11... | collective-permute-start | bytes 638984 | tf_op jit(solution)/shard_map/ppermute | solution.py:73
  19.7 1.3 collective-permute-done
  21.0 1.0 add.8
  22.0 0.0 copy-start
  22.0 14.1 %all_to_all.35 = f32[8,52,128]{2,1,0:T(8,128)S(1)} all-to-all(f32[8,52,128]{2,1,0:T(8,128)S(1)} %add.8), channel_id=1, replica_groups={{0,2,4,6,8,10,12,14},{1,3,5,7,9,11,13,15},{16,18,20,22,24,26,28,30},{17..., dimensions={0} | all-to-all | bytes 425984 | tf_op jit(solution)/shard_map/all_to_all | solution.py:58
  36.1 0.0 copy-start.1
  36.2 12.9 %all_to_all.36.mine = f32[8,52,128]{2,1,0:T(8,128)S(1)} all-to-all(f32[8,52,128]{2,1,0:T(8,128)S(1)} %broadcast_in_dim.9), channel_id=1, replica_groups={{0,2,4,6,8,10,12,14},{1,3,5,7,9,11,13,15},{16,18,20,22,24,26,28,30},{17..., dimensions={0} | all-to-all | bytes 425984 | tf_op jit(solution)/shard_map/all_to_all | solution.py:58
  49.1 3.6 %collective-permute-start.1 = (f32[8,52,128]{2,1,0:T(8,128)S(1)}, f32[8,52,128]{2,1,0:T(8,128)S(1)}, u32[]{:S(2)}, u32[]{:S(2)}) collective-permute-start(f32[8,52,128]{2,1,0:T(8,128)S(1)} %all_to_all.36.mine), channel_id=1, source_target_pairs={{0,1},{1,0},{2,3},{3,2},{4,5},{5,4},{6,7},{7,6},{8,9},{9,8},{10,11... | collective-permute-start | bytes 638984 | tf_op jit(solution)/shard_map/ppermute | solution.py:76
  52.7 1.1 collective-permute-done.1.other
  53.8 0.0 copy-done
  53.8 0.0 copy-done.1
  53.8 1.3 shard_map.68
  55.1 15.1 %all_to_all.37 = f32[8,64,384]{2,1,0:T(8,128)S(1)} all-to-all(f32[8,64,384]{2,1,0:T(8,128)S(1)} %bitcast.5), channel_id=1, replica_groups={{0,16,256,272,512,528,768,784},{32,48,288,304,544,560,800,816},{64,80,3..., dimensions={0} | all-to-all | bytes 1572864 | tf_op jit(solution)/shard_map/all_to_all | solution.py:58
  70.2 23.1 %all_to_all.38 = f32[8,8,384]{2,1,0:T(8,128)S(1)} all-to-all(f32[8,8,384]{2,1,0:T(8,128)S(1)} %bitcast.7), channel_id=1, replica_groups={{0,32,64,96,128,160,192,224},{16,48,80,112,144,176,208,240},{256,288,32..., dimensions={0} | all-to-all | bytes 196608 | tf_op jit(solution)/shard_map/all_to_all | solution.py:58
  93.4 14.9 %all_to_all.39 = f32[8,8,384]{2,1,0:T(8,128)S(1)} all-to-all(f32[8,8,384]{2,1,0:T(8,128)S(1)} %broadcast_in_dim.10), channel_id=1, replica_groups={{0,32,64,96,128,160,192,224},{16,48,80,112,144,176,208,240},{256,288,32..., dimensions={0} | all-to-all | bytes 196608 | tf_op jit(solution)/shard_map/all_to_all | solution.py:58
  108.3 0.1 broadcast_in_dim.11
  108.3 11.7 %all_to_all.40 = f32[8,64,384]{2,1,0:T(8,128)S(1)} all-to-all(f32[8,64,384]{2,1,0:T(8,128)S(1)} %broadcast_in_dim.11), channel_id=1, replica_groups={{0,16,256,272,512,528,768,784},{32,48,288,304,544,560,800,816},{64,80,3..., dimensions={0} | all-to-all | bytes 1572864 | tf_op jit(solution)/shard_map/all_to_all | solution.py:58
  120.1 10.4 %shard_map.69 = (f32[256,256]{1,0:T(8,128)S(1)}, f32[256,512]{1,0:T(8,128)S(1)}, f32[16,1,256]{2,1,0:T(1,128)}) custom-call(f32[512,384]{1,0:T(8,128)S(1)} %bitcast.6), custom_call_target="tpu_custom_call" | custom-call | flops 1000000000 | bytes 2000000 | tf_op jit(solution)/shard_map/pallas_call | solution.py:46
  130.4 9.1 %all-to-all-start.6 = ((f32[16,1,256]{2,1,0:T(1,128)}), f32[16,1,256]{2,1,0:T(1,128)S(1)}, u32[]{:S(2)}, u32[]{:S(2)}) async-start(f32[16,1,256]{2,1,0:T(1,128)} %get-tuple-element.17), calls=%async_computation.6 | async-start | bytes 32768 | tf_op jit(solution)/shard_map/all_to_all | solution.py:58
  139.6 0.0 copy-start.2
  139.6 1.8 %shard_map.70 = (f32[512,256]{1,0:T(8,128)S(1)}, f32[416,512]{1,0:T(8,128)}) custom-call(f32[256,256]{1,0:T(8,128)S(1)} %get-tuple-element.18.inverse, f32[256,416]{1,0:T(8,128)S(1)} %get-tuple-element.19.left_t, f32[256,512]{1,0:T(8,128)S(1)} %get-tuple-element.20.right_t, f32[416,512]{1,0:T(8,128)S(1)} %copy-done, bf16[416,512]{1,0:T(8,128)(2,1)S(1)} %copy-done.1), custom_call_target="tpu_custom_call" | custom-call | flops 1000000000 | bytes 2000000 | tf_op jit(solution)/shard_map/pallas_call | solution.py:46
  141.4 5.6 %all-to-all-done.6.norms = f32[16,1,256]{2,1,0:T(1,128)S(1)} async-done(((f32[16,1,256]{2,1,0:T(1,128)}), f32[16,1,256]{2,1,0:T(1,128)S(1)}, u32[]{:S(2)}, u32[]{:S(2)}) %all-to-all-start.6) | async-done | bytes 16416 | tf_op jit(solution)/shard_map/all_to_all | solution.py:58
  147.0 0.0 copy-done.2
  147.0 1.8 %shard_map.71 = (bf16[416,512]{1,0:T(8,128)(2,1)}, f32[512,256]{1,0:T(8,128)}) custom-call(f32[16,1,256]{2,1,0:T(1,128)S(1)} %all-to-all-done.6.norms, f32[256,256]{1,0:T(8,128)S(1)} %get-tuple-element.18.inverse, f32[256,416]{1,0:T(8,128)S(1)} %get-tuple-element.19.left_t, f32[256,512]{1,0:T(8,128)S(1)} %get-tuple-element.20.right_t, ...), custom_call_target="tpu_custom_call" | custom-call | flops 1000000000 | bytes 2000000 | tf_op jit(solution)/shard_map/pallas_call | solution.py:46
  (5 shorter events, 0.1 us)
Async XLA Ops:
  3.7 17.4 %collective-permute-start = (f32[8,52,128]{2,1,0:T(8,128)}, f32[8,52,128]{2,1,0:T(8,128)S(1)}, u32[]{:S(2)}, u32[]{:S(2)}) collective-permute-start(f32[8,52,128]{2,1,0:T(8,128)} %get-tuple-element.15), channel_id=1, source_target_pairs={{0,1},{1,0},{2,3},{3,2},{4,5},{5,4},{6,7},{7,6},{8,9},{9,8},{10,11... | collective-permute-start | bytes 638984 | tf_op jit(solution)/shard_map/ppermute | solution.py:73
  22.0 31.8 %copy-start = (f32[416,512]{1,0:T(8,128)S(1)}, f32[416,512]{1,0:T(8,128)}, u32[]{:S(2)}) copy-start(f32[416,512]{1,0:T(8,128)} %momentum.5) | copy-start | bytes 2555908
  36.1 17.7 %copy-start.1 = (bf16[416,512]{1,0:T(8,128)(2,1)S(1)}, bf16[416,512]{1,0:T(8,128)(2,1)}, u32[]{:S(2)}) copy-start(bf16[416,512]{1,0:T(8,128)(2,1)} %gradient.5) | copy-start | bytes 1277956
  49.1 4.7 %collective-permute-start.1 = (f32[8,52,128]{2,1,0:T(8,128)S(1)}, f32[8,52,128]{2,1,0:T(8,128)S(1)}, u32[]{:S(2)}, u32[]{:S(2)}) collective-permute-start(f32[8,52,128]{2,1,0:T(8,128)S(1)} %all_to_all.36.mine), channel_id=1, source_target_pairs={{0,1},{1,0},{2,3},{3,2},{4,5},{5,4},{6,7},{7,6},{8,9},{9,8},{10,11... | collective-permute-start | bytes 638984 | tf_op jit(solution)/shard_map/ppermute | solution.py:76
  130.4 16.6 %all-to-all-start.6 = ((f32[16,1,256]{2,1,0:T(1,128)}), f32[16,1,256]{2,1,0:T(1,128)S(1)}, u32[]{:S(2)}, u32[]{:S(2)}) async-start(f32[16,1,256]{2,1,0:T(1,128)} %get-tuple-element.17), calls=%async_computation.6 | async-start | bytes 32768 | tf_op jit(solution)/shard_map/all_to_all | solution.py:58
  139.6 7.4 %copy-start.2 = (bf16[416,512]{1,0:T(8,128)(2,1)S(1)}, bf16[416,512]{1,0:T(8,128)(2,1)}, u32[]{:S(2)}) copy-start(bf16[416,512]{1,0:T(8,128)(2,1)} %weights.1) | copy-start | bytes 1277956
